TPU v7x, 32 devices: a whole 2x2x4 slice. The times are simulated.
32 devices in a mesh: gx: 8 (over y, x, core), gy: 4 (over z).
Axes of the slice: x: 2, y: 2, z: 4, core: 2. Of those that a mesh axis runs over, the one named last changes fastest.
Arguments:
- sources: bfloat16 [8, 4, 8, 64, 256], P('gx', 'gy'), may hold values from -12 to 12
- geometry: bfloat16 [8, 4, 8, 4, 256], P('gx', 'gy'), may hold values from -0.5 to 0.5, as said below
- near_lists: int32 [8, 4, 8, 24], P('gx', 'gy'), may hold values from -1 to 255, as said below
- far_lists: int32 [8, 4, 4, 16], P('gx', 'gy'), may hold values from 0 to 7, as said below
- bases_in: bfloat16 [8, 4, 4, 32, 8, 256], P('gx', 'gy')
- bases_out: bfloat16 [8, 4, 4, 32, 8, 256], P('gx', 'gy'), may hold values from -0.25 to 0.25
- couplings: float32 [8, 4, 4, 32, 512], P('gx', 'gy')
Outputs:
- potential: float32 [8, 4, 8, 64, 256], P('gx', 'gy')
Inputs may be any that keep to these rules, and one draw needn't show every extreme that they name: `near_lists`: for each leaf the first c entries are live, c between 1 and 24 and equal to 24 on some leaves and to 1 on others; the first is the leaf itself, and every live entry names a leaf on a device whose gx and gy indices differ from the leaf's by at most one, in a slot that differs from the leaf's slot by at most one; the other entries are -1. `far_lists`: level 0 entries are below 4, levels 1 and 2 below 8, level 3 below 2. `geometry`: rows 0 to 2 lie in [-0.5, 0.5], row 3 about 0.006 to 0.04.
All inputs are finite; a program needn't handle non-finite values.
Results may differ from a plain program's by a relative error of at most 0.0029.
Values may be sent and summed in bfloat16 or wider, within the bound.
A program may use at most 64 MiB of HBM per device.

v0:
```python
import functools
import math

import jax
import jax.numpy as jnp
from jax import lax
from jax.experimental import pallas as pl
from jax.experimental.pallas import tpu as pltpu
from jax.sharding import PartitionSpec as P

FOUR_PI = 4.0 * math.pi
MESH = pl.DeviceIdType.MESH
UNROLL = 2


def exchange_kernel(
    n_gx, n_gy, packed, proj, coup, far, halo, target,
    col_buf, row_src, row_buf, tab3, gath, int_src, int_buf, c3_src, c3_buf,
    halo_s, halo_r, p1_s, p1_r, p2_s, p2_r, p3_s, p3_r, p4_s, p4_r,
):
    x = lax.axis_index("gx")
    y = lax.axis_index("gy")
    barrier = pltpu.get_barrier_semaphore()

    def inside(dx, dy):
        tests = []
        if dx == -1:
            tests.append(x > 0)
        if dx == 1:
            tests.append(x < n_gx - 1)
        if dy == -1:
            tests.append(y > 0)
        if dy == 1:
            tests.append(y < n_gy - 1)
        return functools.reduce(jnp.logical_and, tests)

    offsets = [(dx, dy) for dx in (-1, 0, 1) for dy in (-1, 0, 1) if (dx, dy) != (0, 0)]
    direct = [o for o in offsets if o[0] * o[1] == 0]
    diagonal = [o for o in offsets if o[0] * o[1] != 0]
    for k in range(1, n_gx):
        pl.semaphore_signal(
            barrier, inc=1, device_id=(lax.rem(x + k, n_gx), y), device_id_type=MESH
        )
    for k in range(1, n_gy):
        pl.semaphore_signal(
            barrier, inc=1, device_id=(x, lax.rem(y + k, n_gy)), device_id_type=MESH
        )
    pl.semaphore_wait(barrier, n_gx - 1 + n_gy - 1)

    def remote(src, dst, send, recv, where):
        return pltpu.make_async_remote_copy(
            src_ref=src, dst_ref=dst, send_sem=send, recv_sem=recv,
            device_id=where, device_id_type=MESH,
        )

    def column(src, buf, send, recv):
        for k in range(1, n_gy):
            to = lax.rem(y + k, n_gy)
            remote(src, buf.at[y], send.at[k], recv.at[y], (x, to)).start()
        buf[y] = src[...]

    def column_wait(src, buf, send, recv):
        for k in range(1, n_gy):
            peer = lax.rem(y + k, n_gy)
            remote(src, buf.at[peer], send.at[k], recv.at[peer], (x, peer)).wait_recv()

    def slot(dx, dy):
        return (dx + 1) * 3 + dy + 1

    def halo_copy(dx, dy):
        block = halo.at[slot(0, dy)] if dx != 0 and dy != 0 else packed
        there = slot(-dx, dy) if dx != 0 else slot(0, -dy)
        return remote(
            block, halo.at[there], halo_s.at[slot(dx, dy)], halo_r.at[there],
            (x + dx, y + dy if dx == 0 else y),
        )

    def halo_start(dx, dy):
        @pl.when(inside(dx, dy))
        def _():
            halo_copy(dx, dy).start()

    def halo_arrived(dx, dy):
        @pl.when(inside(dx, dy))
        def _():
            at = slot(dx, dy)
            origin = (x + dx, y) if dx != 0 else (x, y + dy)
            remote(packed, halo.at[at], halo_s.at[at], halo_r.at[at], origin).wait_recv()

    column(proj, col_buf, p1_s, p1_r)
    for dx, dy in direct:
        halo_start(dx, dy)
    halo[4] = packed[...]

    column_wait(proj, col_buf, p1_s, p1_r)
    quarter = 4 * (y // 4)
    half = target.shape[1]
    row_src[0:32, 0:half] = sum(col_buf[quarter + g, 32:64, 0:half] for g in range(4))
    coarse = sum(col_buf[g, :, half:] for g in range(n_gy))
    row_src[0:32, half:] = coarse[0:32]
    row_src[32:48, 0:half] = coarse[32:48]
    row_src[32:48, half:] = coarse[48:64]
    for k in range(1, n_gx):
        to = lax.rem(x + k, n_gx)
        remote(row_src, row_buf.at[x], p2_s.at[k], p2_r.at[x], (to, y)).start()
    row_buf[x] = row_src[...]
    for m in range(16):
        gath[pl.ds(m * 32, 32), :] = col_buf[far[0, m], 0:32, 0:half]
    first = jnp.dot(
        coup[0], gath[...], preferred_element_type=jnp.float32, precision=lax.Precision.HIGHEST
    )
    target[0:32, :] = first.astype(jnp.bfloat16)
    for k in range(1, n_gx):
        peer = lax.rem(x + k, n_gx)
        remote(row_src, row_buf.at[peer], p2_s.at[k], p2_r.at[peer], (peer, y)).wait_recv()
    for dy in (-1, 1):
        halo_arrived(0, dy)
    for dx, dy in diagonal:
        halo_start(dx, dy)
    for c in range(n_gx // 4):
        coarse = sum(row_buf[4 * c + g, 32:48, :] for g in range(4))
        tab3[c, 0:16, :] = coarse[:, 0:half]
        tab3[c, 16:32, :] = coarse[:, half:]
    for level in (1, 2, 3):
        for m in range(16):
            s = far[level, m]
            if level == 3:
                gath[pl.ds(m * 32, 32), :] = tab3[s]
            elif level == 1:
                gath[pl.ds(m * 32, 32), :] = row_buf[s, 0:32, 0:half]
            else:
                gath[pl.ds(m * 32, 32), :] = row_buf[s, 0:32, half:]
        term = jnp.dot(
            coup[level], gath[...], preferred_element_type=jnp.float32,
            precision=lax.Precision.HIGHEST,
        )
        if level == 1:
            int_src[0:32, 0:half] = term
        elif level == 2:
            int_src[0:32, half:] = term
        else:
            int_src[32:48, 0:half] = term[0:16]
            int_src[32:48, half:] = term[16:32]
    column(int_src, int_buf, p3_s, p3_r)
    column_wait(int_src, int_buf, p3_s, p3_r)
    c3_src[...] = sum(int_buf[g, 32:48, :] for g in range(n_gy))
    base = 4 * (x // 4)
    spot = lax.rem(x, 4)
    for k in range(1, 4):
        to = base + lax.rem(spot + k, 4)
        remote(c3_src, c3_buf.at[spot], p4_s.at[k], p4_r.at[spot], (to, y)).start()
    c3_buf[spot] = c3_src[...]
    target[32:64, :] = sum(int_buf[quarter + g, 0:32, 0:half] for g in range(4)).astype(jnp.bfloat16)
    target[64:96, :] = sum(int_buf[g, 0:32, half:] for g in range(n_gy)).astype(jnp.bfloat16)
    for k in range(1, 4):
        peer = lax.rem(spot + k, 4)
        remote(c3_src, c3_buf.at[peer], p4_s.at[k], p4_r.at[peer], (base + peer, y)).wait_recv()
    coarse = sum(c3_buf[g] for g in range(4)).astype(jnp.bfloat16)
    target[96:112, :] = coarse[:, 0:half]
    target[112:128, :] = coarse[:, half:]

    for dx, dy in offsets:
        if dx != 0:
            halo_arrived(dx, dy)

        @pl.when(inside(dx, dy))
        def _():
            halo_copy(dx, dy).wait_send()

    for k in range(1, n_gy):
        to = lax.rem(y + k, n_gy)
        remote(proj, col_buf.at[y], p1_s.at[k], p1_r.at[y], (x, to)).wait_send()
        remote(int_src, int_buf.at[y], p3_s.at[k], p3_r.at[y], (x, to)).wait_send()
    for k in range(1, n_gx):
        to = lax.rem(x + k, n_gx)
        remote(row_src, row_buf.at[x], p2_s.at[k], p2_r.at[x], (to, y)).wait_send()
    for k in range(1, 4):
        to = base + lax.rem(spot + k, 4)
        remote(c3_src, c3_buf.at[spot], p4_s.at[k], p4_r.at[spot], (to, y)).wait_send()


def exchange(packed, proj, coup, far, n_gx, n_gy):
    rows, panels = packed.shape
    rhs = proj.shape[1] // 2
    vmem = pl.BlockSpec(memory_space=pltpu.VMEM)
    f32 = jnp.float32
    sems = pltpu.SemaphoreType.DMA
    return pl.pallas_call(
        functools.partial(exchange_kernel, n_gx, n_gy),
        out_shape=(
            jax.ShapeDtypeStruct((9, rows, panels), jnp.bfloat16),
            jax.ShapeDtypeStruct((128, rhs), jnp.bfloat16),
        ),
        in_specs=[vmem, vmem, vmem, pl.BlockSpec(memory_space=pltpu.SMEM)],
        out_specs=(vmem, vmem),
        scratch_shapes=[
            pltpu.VMEM((n_gy, 64, 2 * rhs), f32),
            pltpu.VMEM((48, 2 * rhs), f32),
            pltpu.VMEM((n_gx, 48, 2 * rhs), f32),
            pltpu.VMEM((n_gx // 4, 32, rhs), f32),
            pltpu.VMEM((512, rhs), f32),
            pltpu.VMEM((48, 2 * rhs), f32),
            pltpu.VMEM((n_gy, 48, 2 * rhs), f32),
            pltpu.VMEM((16, 2 * rhs), f32),
            pltpu.VMEM((4, 16, 2 * rhs), f32),
            sems((9,)), sems((9,)),
            sems((n_gy,)), sems((n_gy,)),
            sems((n_gx,)), sems((n_gx,)),
            sems((n_gy,)), sems((n_gy,)),
            sems((4,)), sems((4,)),
        ],
        compiler_params=pltpu.CompilerParams(
            collective_id=0, has_side_effects=True, vmem_limit_bytes=32 * 1024 * 1024
        ),
    )(packed, proj, coup, far)


def near_kernel(slots, leaf_dev, index, shift, count, live, halo, tfeat, out, sfeat, scale):
    leaf = pl.program_id(0)
    rhs = out.shape[1]

    @pl.when(leaf == 0)
    def _():
        def source_features(place, carry):
            def row(c):
                wide = halo[place, pl.ds(leaf_dev * rhs, 4 * leaf_dev), :].astype(jnp.float32)
                return wide[c * leaf_dev : (c + 1) * leaf_dev]

            sx, sy, sz, area = row(0), row(1), row(2), row(3)
            dx = (place // 3 - 1).astype(jnp.float32)
            dy = (lax.rem(place, 3) - 1).astype(jnp.float32)
            q = (sx + dx) * (sx + dx) + (sy + dy) * (sy + dy) + sz * sz + area
            high = q.astype(jnp.bfloat16).astype(jnp.float32)
            mid = (q - high).astype(jnp.bfloat16).astype(jnp.float32)
            one, zero = jnp.ones_like(q), jnp.zeros_like(q)
            rows = [sx, sy, sz, dx + zero, dy + zero, sz, one, one, one]
            rows += [high, mid, q - high - mid] + [zero] * 4
            own = pl.ds(pl.multiple_of(place * leaf_dev, leaf_dev), leaf_dev)
            for k, value in enumerate(rows):
                sfeat[own, k, :] = value
            scale[own, :] = area * (1.0 / FOUR_PI)
            return carry

        lax.fori_loop(0, 9, source_features, 0)

    out[0] = jnp.zeros(out.shape[1:], jnp.float32)

    def step(pair, carry):
        total = None
        for u in range(UNROLL):
            at = leaf * slots + pair * UNROLL + u
            n = index[at]
            squared = lax.dot_general(
                tfeat[0, shift[at]], sfeat[n].astype(jnp.bfloat16), (((0,), (0,)), ((), ())),
                preferred_element_type=jnp.float32,
            )
            weight = scale[pl.ds(n, 1), :] * live[at].astype(jnp.float32)
            kernel = (lax.rsqrt(squared) * weight).astype(jnp.bfloat16)
            src = halo[n // 8, pl.ds(pl.multiple_of(lax.rem(n, 8) * rhs, rhs), rhs), :]
            term = lax.dot_general(
                src, kernel, (((1,), (1,)), ((), ())), preferred_element_type=jnp.float32
            )
            total = term if total is None else total + term
        out[0] += total
        return carry

    lax.fori_loop(0, (count[leaf] + UNROLL - 1) // UNROLL, step, 0)


def pieces(v):
    high = lax.reduce_precision(v, 8, 7)
    rest = v - high
    mid = lax.reduce_precision(rest, 8, 7)
    return [high, mid, lax.reduce_precision(rest - mid, 8, 7)]


def near(halo, tfeat, index, shift, count, live, leaf_dev, rhs, slots):
    panels = halo.shape[2]
    whole = lambda *shape: pl.BlockSpec(shape, lambda l, *_: (0,) * len(shape))
    return pl.pallas_call(
        functools.partial(near_kernel, slots, leaf_dev),
        out_shape=jax.ShapeDtypeStruct((leaf_dev, rhs, panels), jnp.float32),
        grid_spec=pltpu.PrefetchScalarGridSpec(
            num_scalar_prefetch=4,
            grid=(leaf_dev,),
            in_specs=[
                whole(*halo.shape),
                pl.BlockSpec((1, 3, 16, panels), lambda l, *_: (l, 0, 0, 0)),
            ],
            out_specs=pl.BlockSpec((1, rhs, panels), lambda l, *_: (l, 0, 0)),
            scratch_shapes=[
                pltpu.VMEM((9 * leaf_dev, 16, panels), jnp.float32),
                pltpu.VMEM((9 * leaf_dev, panels), jnp.float32),
            ],
        ),
        compiler_params=pltpu.CompilerParams(vmem_limit_bytes=32 * 1024 * 1024),
    )(index, shift, count, live, halo, tfeat)


def body(sources, geometry, near_lists, far_lists, bases_in, bases_out, couplings):
    leaf_dev, rhs, panels = sources.shape[2:]
    slots = near_lists.shape[3]
    n_gx, n_gy = lax.axis_size("gx"), lax.axis_size("gy")
    row_pos, col_pos = lax.axis_index("gx"), lax.axis_index("gy")
    geo = geometry[0, 0]
    by_row = jnp.transpose(geo, (1, 0, 2)).reshape(4 * leaf_dev, panels)
    packed = jnp.concatenate([sources.reshape(leaf_dev * rhs, panels), by_row], axis=0)
    projection = jnp.einsum(
        "aqlp,lrp->aqr", bases_in[0, 0], sources[0, 0], preferred_element_type=jnp.float32
    )
    level_pairs = projection.reshape(2, 64, rhs)
    halo, target = exchange(
        packed, jnp.concatenate([level_pairs[0], level_pairs[1]], axis=1), couplings[0, 0], far_lists[0, 0], n_gx, n_gy
    )

    lists = near_lists[0, 0]
    live = lists >= 0
    own_leaf = jnp.arange(leaf_dev, dtype=jnp.int32)
    device = lists // leaf_dev
    src_leaf = lists % leaf_dev
    local = ((device // n_gy - row_pos + 1) * 3 + device % n_gy - col_pos + 1) * leaf_dev + src_leaf
    index = jnp.where(live, local, 4 * leaf_dev + own_leaf[:, None])
    shift = jnp.where(live, src_leaf - own_leaf[:, None] + 1, 1)
    count = jnp.sum(live.astype(jnp.int32), axis=1)

    t = geo.astype(jnp.float32)[:, None]
    tx, ty, tz = t[:, :, 0], t[:, :, 1], t[:, :, 2]
    dz = jnp.arange(-1, 2, dtype=jnp.float32)[None, :, None]
    shape = (leaf_dev, 3, panels)
    full = lambda v: jnp.broadcast_to(v, shape)
    one, zero = jnp.ones(shape, jnp.float32), jnp.zeros(shape, jnp.float32)
    p = tx * tx + ty * ty + (tz - dz) * (tz - dz)
    tfeat = jnp.stack(
        [full(v) for v in (-2 * tx, -2 * ty, -2 * tz, -2 * tx, -2 * ty, 2 * dz)]
        + pieces(p) + [one] * 3 + [zero] * 4,
        axis=2,
    ).astype(jnp.bfloat16)

    near_field = near(
        halo, tfeat,
        index.reshape(-1), shift.reshape(-1), count, live.astype(jnp.int32).reshape(-1),
        leaf_dev, rhs, slots,
    )
    far_field = jnp.einsum(
        "aqr,aqlp->lrp", target.reshape(4, 32, rhs), bases_out[0, 0],
        preferred_element_type=jnp.float32,
    )
    return (near_field + far_field).reshape(sources.shape)


def solution(mesh):
    in_specs = (
        P("gx", "gy", None, None, None),
        P("gx", "gy", None, None, None),
        P("gx", "gy", None, None),
        P("gx", "gy", None, None),
        P("gx", "gy", None, None, None, None),
        P("gx", "gy", None, None, None, None),
        P("gx", "gy", None, None, None),
    )
    out_specs = P("gx", "gy", None, None, None)
    return jax.shard_map(body, mesh=mesh, in_specs=in_specs, out_specs=out_specs, check_vma=False)
```

profile of v0, /device:TPU:23, one launch (start us, length us, event | category | flops | bytes accessed | tf_op | source)
XLA Modules:
  0.0 70.4 jit_solution(14875074460234506596)
XLA Ops:
  0.0 0.0 copy-start
  0.0 0.0 copy-start.1
  0.0 0.0 copy-start.2
  0.0 1.0 %copy-done = bf16[1,1,4,32,8,256]{5,4,3,2,1,0:T(8,128)(2,1)S(1)} copy-done((bf16[1,1,4,32,8,256]{5,4,3,2,1,0:T(8,128)(2,1)S(1)}, bf16[1,1,4,32,8,256]{5,4,3,2,1,0:T(8,128)(2,1)}, u32[]{:S(2)}) %copy-start) | copy-done | bytes 524312
  1.0 0.8 %convert_reduce_fusion.count = s32[8]{0:T(128)S(1)} fusion(s32[1,1,8,24]{3,2,1,0:T(8,128)} %param.9), kind=kLoop, calls=%fused_computation.25 | loop fusion | flops 568 | bytes 800 | tf_op jit(solution)/shard_map/reduce_sum | solution.py:324
  1.9 0.8 %squeeze.32 = s32[192]{0:T(256)S(1)} reshape(s32[1,1,8,24]{3,2,1,0:T(8,128)} %param.9) | data formatting | bytes 1536 | tf_op jit(solution)/shard_map/squeeze | solution.py:316
  2.6 0.1 broadcast_in_dim.16
  2.7 0.1 broadcast_in_dim.17
  2.8 0.1 sub.101
  2.9 0.7 %copy.29 = bf16[4,8,256]{2,1,0:T(8,128)(2,1)S(1)} copy(bf16[4,8,256]{2,0,1:T(4,128)(2,1)} %bitcast.58) | data formatting | bytes 32768 | tf_op jit(solution)/shard_map/transpose | solution.py:306
  3.6 0.1 stack_broadcast_in_dim.13
  3.7 0.7 %bitcast_convert_fusion = f32[8,1,4,256]{3,0,2,1:T(8,128)S(1)} fusion(bf16[1,1,8,4,256]{4,3,2,1,0:T(4,128)(2,1)} %param.8), kind=kLoop, calls=%fused_computation.16 | loop fusion | flops 8192 | bytes 49152 | tf_op jit(solution)/shard_map/convert_element_type | solution.py:326
  4.5 0.1 fusion.6
  4.8 0.4 stack.15.tfeat
  5.2 1.4 %convolution_bitcast_fusion.1 = f32[4,32,64]{2,1,0:T(8,128)S(1)} fusion(bf16[4,32,8,256]{3,2,1,0:T(8,128)(2,1)} %bitcast.60, bf16[1,1,8,64,256]{4,3,2,1,0:T(8,128)(2,1)} %param.7), kind=kOutput, calls=%fused_computation.3 | convolution fusion | flops 33554432 | bytes 819200 | tf_op jit(solution)/shard_map/aqlp,lrp->aqr/dot_general | solution.py:308
  6.6 0.1 pad_maximum_fusion.1.proj
  6.7 1.0 %pad_maximum_fusion.packed = bf16[544,256]{1,0:T(8,128)(2,1)S(1)} fusion(bf16[32,256]{1,0:T(8,128)(2,1)S(1)} %bitcast.59, bf16[512,256]{1,0:T(8,128)(2,1)} %bitcast.55), kind=kLoop, calls=%fused_computation.6 | loop fusion | flops 557056 | bytes 557056 | tf_op jit(solution)/shard_map/concatenate | solution.py:307
  7.7 0.0 copy-done.1
  7.7 0.0 copy-done.2
  7.7 26.9 %shard_map.73 = (bf16[9,544,256]{2,1,0:T(8,128)(2,1)S(1)}, bf16[128,64]{1,0:T(8,128)(2,1)S(1)}) custom-call(bf16[544,256]{1,0:T(8,128)(2,1)S(1)} %pad_maximum_fusion.packed, f32[64,128]{1,0:T(8,128)S(1)} %pad_maximum_fusion.1.proj, f32[4,32,512]{2,1,0:T(8,128)S(1)} %bitcast.52, s32[4,16]{1,0:T(4,128)S(1)} %bitcast.54), custom_call_target="tpu_custom_call" | custom-call | tf_op jit(solution)/shard_map/pallas_call | solution.py:188
  34.7 34.7 %shard_map.74 = f32[8,64,256]{2,1,0:T(8,128)S(1)} custom-call(s32[192]{0:T(256)S(1)} %get-tuple-element.20.index, s32[192]{0:T(256)S(1)} %get-tuple-element.19.shift, s32[8]{0:T(128)S(1)} %convert_reduce_fusion.count, s32[192]{0:T(256)S(1)} %fusion.10.live, bf16[9,544,256]{2,1,0:T(8,128)(2,1)S(1)} %get-tuple-element.7.halo, ...), custom_call_target="tpu_custom_call" | custom-call | tf_op jit(solution)/shard_map/pallas_call | solution.py:280
  69.4 1.1 %fusion.1 = f32[1,1,8,64,256]{4,3,2,1,0:T(8,128)} fusion(f32[8,64,256]{2,1,0:T(8,128)S(1)} %shard_map.74, bf16[4,32,64,1]{2,1,0,3:T(8,128)(2,1)S(1)} %bitcast.53, bf16[4,32,8,256]{3,2,1,0:T(8,128)(2,1)S(1)} %bitcast.51), kind=kOutput, calls=%fused_computation.2 | convolution fusion | flops 33685504 | bytes 1589248 | tf_op jit(solution)/shard_map/aqr,aqlp->lrp/dot_general | solution.py:344
  (16 shorter events, 0.2 us)
Async XLA Ops:
  0.0 1.0 %copy-start = (bf16[1,1,4,32,8,256]{5,4,3,2,1,0:T(8,128)(2,1)S(1)}, bf16[1,1,4,32,8,256]{5,4,3,2,1,0:T(8,128)(2,1)}, u32[]{:S(2)}) copy-start(bf16[1,1,4,32,8,256]{5,4,3,2,1,0:T(8,128)(2,1)} %param.12) | copy-start | bytes 1572868
  0.0 7.7 %copy-start.1 = (f32[1,1,4,32,512]{4,3,2,1,0:T(8,128)S(1)}, f32[1,1,4,32,512]{4,3,2,1,0:T(8,128)}, u32[]{:S(2)}) copy-start(f32[1,1,4,32,512]{4,3,2,1,0:T(8,128)} %param.13) | copy-start | bytes 786436
  0.0 7.7 %copy-start.2 = (s32[1,1,4,16]{3,2,1,0:T(4,128)S(1)}, s32[1,1,4,16]{3,2,1,0:T(4,128)}, u32[]{:S(2)}) copy-start(s32[1,1,4,16]{3,2,1,0:T(4,128)} %param.10) | copy-start | bytes 772
where the time goes:
time: 69.7 us; the launch traced here: 70.4 us
  Pallas kernels  61.7 us (89%)
  local copies, waits for them, and re-layouts  3.37 us (5%)
  other arithmetic  2.81 us (4%)
  matrix products  2.45 us (4%)
    pallas_call x1, Pallas kernels, near(): pl.pallas_call(functools.partial(near_kernel, slots, leaf_dev), out_shape...  34.7 us
    pallas_call x1, Pallas kernels, exchange(): pl.pallas_call(functools.partial(exchange_kernel, n_gx, n_gy), out_shape=...  26.9 us
    dot_general x1, matrix products, body(): jnp.einsum('aqlp,lrp->aqr', bases_in[0, 0], sources[0, 0], preferred_elem...  1.39 us

commit v1 on v0

--- a/solution.py
+++ b/solution.py
@@ -10,7 +10,8 @@
 
 FOUR_PI = 4.0 * math.pi
 MESH = pl.DeviceIdType.MESH
-UNROLL = 2
+UNROLL = 4
+FEATURES = 32
 
 
 def exchange_kernel(
@@ -215,7 +216,7 @@
     )(packed, proj, coup, far)
 
 
-def near_kernel(slots, leaf_dev, index, shift, count, live, halo, tfeat, out, sfeat, scale):
+def near_kernel(slots, leaf_dev, index, shift, count, live, halo, tfeat, out, sfeat):
     leaf = pl.program_id(0)
     rhs = out.shape[1]
 
@@ -229,16 +230,24 @@
             sx, sy, sz, area = row(0), row(1), row(2), row(3)
             dx = (place // 3 - 1).astype(jnp.float32)
             dy = (lax.rem(place, 3) - 1).astype(jnp.float32)
-            q = (sx + dx) * (sx + dx) + (sy + dy) * (sy + dy) + sz * sz + area
-            high = q.astype(jnp.bfloat16).astype(jnp.float32)
-            mid = (q - high).astype(jnp.bfloat16).astype(jnp.float32)
-            one, zero = jnp.ones_like(q), jnp.zeros_like(q)
-            rows = [sx, sy, sz, dx + zero, dy + zero, sz, one, one, one]
-            rows += [high, mid, q - high - mid] + [zero] * 4
+            sx, sy = sx + dx, sy + dy
+            factor = FOUR_PI / area
+            factor = factor * factor
+
+            def split(v):
+                high = v.astype(jnp.bfloat16).astype(jnp.float32)
+                mid = (v - high).astype(jnp.bfloat16).astype(jnp.float32)
+                return [high, mid, v - high - mid]
+
+            high, mid, low = split(factor)
+            along_z = split(factor * sz)
+            rows = split(factor * sx) + split(factor * sy) + along_z + along_z
+            rows += [high, high, high, mid, mid, low]
+            rows += split(factor * (sx * sx + sy * sy + sz * sz + area))
+            rows += [jnp.zeros_like(factor)] * (FEATURES - len(rows))
             own = pl.ds(pl.multiple_of(place * leaf_dev, leaf_dev), leaf_dev)
             for k, value in enumerate(rows):
                 sfeat[own, k, :] = value
-            scale[own, :] = area * (1.0 / FOUR_PI)
             return carry
 
         lax.fori_loop(0, 9, source_features, 0)
@@ -251,14 +260,14 @@
             at = leaf * slots + pair * UNROLL + u
             n = index[at]
             squared = lax.dot_general(
-                tfeat[0, shift[at]], sfeat[n].astype(jnp.bfloat16), (((0,), (0,)), ((), ())),
+                sfeat[n].astype(jnp.bfloat16), tfeat[0, shift[at]], (((0,), (0,)), ((), ())),
                 preferred_element_type=jnp.float32,
             )
-            weight = scale[pl.ds(n, 1), :] * live[at].astype(jnp.float32)
-            kernel = (lax.rsqrt(squared) * weight).astype(jnp.bfloat16)
+            kernel = lax.rsqrt(squared).astype(jnp.bfloat16)
             src = halo[n // 8, pl.ds(pl.multiple_of(lax.rem(n, 8) * rhs, rhs), rhs), :]
             term = lax.dot_general(
-                src, kernel, (((1,), (1,)), ((), ())), preferred_element_type=jnp.float32
+                src * live[at].astype(jnp.bfloat16), kernel, (((1,), (0,)), ((), ())),
+                preferred_element_type=jnp.float32,
             )
             total = term if total is None else total + term
         out[0] += total
@@ -285,12 +294,11 @@
             grid=(leaf_dev,),
             in_specs=[
                 whole(*halo.shape),
-                pl.BlockSpec((1, 3, 16, panels), lambda l, *_: (l, 0, 0, 0)),
+                pl.BlockSpec((1, 3, FEATURES, panels), lambda l, *_: (l, 0, 0, 0)),
             ],
             out_specs=pl.BlockSpec((1, rhs, panels), lambda l, *_: (l, 0, 0)),
             scratch_shapes=[
-                pltpu.VMEM((9 * leaf_dev, 16, panels), jnp.float32),
-                pltpu.VMEM((9 * leaf_dev, panels), jnp.float32),
+                pltpu.VMEM((9 * leaf_dev, FEATURES, panels), jnp.float32),
             ],
         ),
         compiler_params=pltpu.CompilerParams(vmem_limit_bytes=32 * 1024 * 1024),
@@ -330,11 +338,11 @@
     full = lambda v: jnp.broadcast_to(v, shape)
     one, zero = jnp.ones(shape, jnp.float32), jnp.zeros(shape, jnp.float32)
     p = tx * tx + ty * ty + (tz - dz) * (tz - dz)
-    tfeat = jnp.stack(
-        [full(v) for v in (-2 * tx, -2 * ty, -2 * tz, -2 * tx, -2 * ty, 2 * dz)]
-        + pieces(p) + [one] * 3 + [zero] * 4,
-        axis=2,
-    ).astype(jnp.bfloat16)
+    high, mid, low = pieces(p)
+    rows = [full(-2 * tx)] * 3 + [full(-2 * ty)] * 3 + [full(-2 * tz)] * 3 + [full(2 * dz)] * 3
+    rows += [high, mid, low, high, mid, high] + [one] * 3
+    rows += [zero] * (FEATURES - len(rows))
+    tfeat = jnp.stack(rows, axis=2).astype(jnp.bfloat16)
 
     near_field = near(
         halo, tfeat,

time: 69.7 us -> 57.5 us (0.82)
  the two profiles are of different devices: /device:TPU:23 before, /device:TPU:17 now
where the time goes in v1:
time: 57.5 us; the launch traced here: 56.9 us
  Pallas kernels  48.7 us (85%)
  local copies, waits for them, and re-layouts  3.77 us (7%)
  matrix products  2.44 us (4%)
  other arithmetic  1.86 us (3%)
    pallas_call x1, Pallas kernels, exchange(): pl.pallas_call(functools.partial(exchange_kernel, n_gx, n_gy), out_shape=...  28 us
    pallas_call x1, Pallas kernels, near(): pl.pallas_call(functools.partial(near_kernel, slots, leaf_dev), out_shape...  20.6 us
    dot_general x1, matrix products, body(): jnp.einsum('aqlp,lrp->aqr', bases_in[0, 0], sources[0, 0], preferred_elem...  1.39 us

profile of v1, /device:TPU:17, one launch (start us, length us, event | category | flops | bytes accessed | tf_op | source)
XLA Modules:
  0.0 56.9 jit_solution(8330168474026814899)
XLA Ops:
  0.0 0.0 copy-start
  0.0 0.0 copy-start.3
  0.0 0.0 copy-start.1
  0.0 0.0 copy-start.2
  0.0 1.0 %copy-done = bf16[1,1,4,32,8,256]{5,4,3,2,1,0:T(8,128)(2,1)S(1)} copy-done((bf16[1,1,4,32,8,256]{5,4,3,2,1,0:T(8,128)(2,1)S(1)}, bf16[1,1,4,32,8,256]{5,4,3,2,1,0:T(8,128)(2,1)}, u32[]{:S(2)}) %copy-start) | copy-done | bytes 524312
  1.0 0.8 %convert_reduce_fusion.count = s32[8]{0:T(128)S(1)} fusion(s32[1,1,8,24]{3,2,1,0:T(8,128)} %param.9), kind=kLoop, calls=%fused_computation.25 | loop fusion | flops 568 | bytes 800 | tf_op jit(solution)/shard_map/reduce_sum | solution.py:332
  1.9 0.8 %squeeze.32 = s32[192]{0:T(256)S(1)} reshape(s32[1,1,8,24]{3,2,1,0:T(8,128)} %param.9) | data formatting | bytes 1536 | tf_op jit(solution)/shard_map/squeeze | solution.py:324
  2.6 0.1 broadcast_in_dim.16
  2.7 0.1 broadcast_in_dim.17
  2.8 0.1 sub.101
  2.9 0.7 %copy.29 = bf16[4,8,256]{2,1,0:T(8,128)(2,1)S(1)} copy(bf16[4,8,256]{2,0,1:T(4,128)(2,1)} %bitcast.58) | data formatting | bytes 32768 | tf_op jit(solution)/shard_map/transpose | solution.py:314
  3.6 0.1 stack_broadcast_in_dim.19
  3.7 0.7 %bitcast_convert_fusion = f32[8,1,4,256]{3,0,2,1:T(8,128)S(1)} fusion(bf16[1,1,8,4,256]{4,3,2,1,0:T(4,128)(2,1)} %param.8), kind=kLoop, calls=%fused_computation.16 | loop fusion | flops 8192 | bytes 49152 | tf_op jit(solution)/shard_map/convert_element_type | solution.py:334
  4.5 0.1 fusion.6
  4.7 1.4 %convolution_bitcast_fusion.1 = f32[4,32,64]{2,1,0:T(8,128)S(1)} fusion(bf16[4,32,8,256]{3,2,1,0:T(8,128)(2,1)} %bitcast.60, bf16[1,1,8,64,256]{4,3,2,1,0:T(8,128)(2,1)} %param.7), kind=kOutput, calls=%fused_computation.3 | convolution fusion | flops 33554432 | bytes 819200 | tf_op jit(solution)/shard_map/aqlp,lrp->aqr/dot_general | solution.py:316
  6.1 0.1 pad_maximum_fusion.1.proj
  6.3 0.8 %stack.22.tfeat = bf16[8,3,32,256]{3,2,1,0:T(8,128)(2,1)S(1)} concatenate(bf16[8,3,1,256]{3,2,1,0:T(2,128)(2,1)S(1)} %stack_broadcast_in_dim.16, bf16[8,3,1,256]{3,2,1,0:T(2,128)(2,1)S(1)} %stack_broadcast_in_dim.16, bf16[8,3,1,256]{3,2,1,0:T(2,128)(2,1)S(1)} %stack_broadcast_in_dim.16, bf16[8,3,1,256]{3,2,1,0:T(2,128)(2,1)S(1)} %stack_broadcast_in_dim.17, ...), dimensions={2} | concatenate | bytes 786432 | tf_op jit(solution)/shard_map/stack | solution.py:345
  7.1 0.0 copy-done.3
  7.2 0.0 copy-done.1
  7.2 0.0 copy-done.2
  7.2 28.0 %shard_map.73 = (bf16[9,544,256]{2,1,0:T(8,128)(2,1)S(1)}, bf16[128,64]{1,0:T(8,128)(2,1)S(1)}) custom-call(bf16[544,256]{1,0:T(8,128)(2,1)S(1)} %pad_maximum_fusion.packed, f32[64,128]{1,0:T(8,128)S(1)} %pad_maximum_fusion.1.proj, f32[4,32,512]{2,1,0:T(8,128)S(1)} %bitcast.52, s32[4,16]{1,0:T(4,128)S(1)} %bitcast.54), custom_call_target="tpu_custom_call" | custom-call | tf_op jit(solution)/shard_map/pallas_call | solution.py:189
  35.2 20.6 %shard_map.74 = f32[8,64,256]{2,1,0:T(8,128)S(1)} custom-call(s32[192]{0:T(256)S(1)} %get-tuple-element.20.index, s32[192]{0:T(256)S(1)} %get-tuple-element.19.shift, s32[8]{0:T(128)S(1)} %convert_reduce_fusion.count, s32[192]{0:T(256)S(1)} %fusion.10.live, bf16[9,544,256]{2,1,0:T(8,128)(2,1)S(1)} %get-tuple-element.7.halo, ...), custom_call_target="tpu_custom_call" | custom-call | tf_op jit(solution)/shard_map/pallas_call | solution.py:289
  55.9 1.1 %fusion.1 = f32[1,1,8,64,256]{4,3,2,1,0:T(8,128)} fusion(f32[8,64,256]{2,1,0:T(8,128)S(1)} %shard_map.74, bf16[4,32,64,1]{2,1,0,3:T(8,128)(2,1)S(1)} %bitcast.53, bf16[4,32,8,256]{3,2,1,0:T(8,128)(2,1)S(1)} %bitcast.51), kind=kOutput, calls=%fused_computation.2 | convolution fusion | flops 33685504 | bytes 1589248 | tf_op jit(solution)/shard_map/aqr,aqlp->lrp/dot_general | solution.py:352
  (19 shorter events, 0.3 us)
Async XLA Ops:
  0.0 1.0 %copy-start = (bf16[1,1,4,32,8,256]{5,4,3,2,1,0:T(8,128)(2,1)S(1)}, bf16[1,1,4,32,8,256]{5,4,3,2,1,0:T(8,128)(2,1)}, u32[]{:S(2)}) copy-start(bf16[1,1,4,32,8,256]{5,4,3,2,1,0:T(8,128)(2,1)} %param.12) | copy-start | bytes 1572868
  0.0 7.1 %copy-start.3 = (bf16[1,1,8,64,256]{4,3,2,1,0:T(8,128)(2,1)S(1)}, bf16[1,1,8,64,256]{4,3,2,1,0:T(8,128)(2,1)}, u32[]{:S(2)}) copy-start(bf16[1,1,8,64,256]{4,3,2,1,0:T(8,128)(2,1)} %param.7) | copy-start | bytes 786436
  0.0 7.2 %copy-start.1 = (f32[1,1,4,32,512]{4,3,2,1,0:T(8,128)S(1)}, f32[1,1,4,32,512]{4,3,2,1,0:T(8,128)}, u32[]{:S(2)}) copy-start(f32[1,1,4,32,512]{4,3,2,1,0:T(8,128)} %param.13) | copy-start | bytes 786436
  0.0 7.2 %copy-start.2 = (s32[1,1,4,16]{3,2,1,0:T(4,128)S(1)}, s32[1,1,4,16]{3,2,1,0:T(4,128)}, u32[]{:S(2)}) copy-start(s32[1,1,4,16]{3,2,1,0:T(4,128)} %param.10) | copy-start | bytes 772
